TPU v7x, 512 devices: a whole 4x4x16 slice. The times are simulated.
512 devices in a mesh: seq: 32 (over x, z_lo), head: 8 (over y, core), enc: 2 (over z_hi).
Axes of the slice: x: 4, y: 4, z: 16 (z_hi: 2, z_lo: 8; z = z_hi * 8 + z_lo), core: 2. Of those that a mesh axis runs over, the one named last changes fastest.
Arguments:
- queries: bfloat16 [10240, 4096], P('seq', ('head', 'enc')), may hold values from -2000 to 2000
- keys: bfloat16 [10240, 4096], P('seq', ('head', 'enc')), may hold values from -2000 to 2000
- values: bfloat16 [10240, 4096], P('seq', ('head', 'enc')), may hold values from -6 to 6
- out_weight: bfloat16 [4096, 5120], P(('head', 'enc'), 'seq'), may hold values from -0.1875 to 0.1875
- q_gain: float32 [4096], P(('head', 'enc')), may hold values from 0.75 to 3
- k_gain: float32 [4096], P(('head', 'enc')), may hold values from 0.75 to 3
- gate: float32 [5120], P(('head', 'enc')), may hold values from 1 to 8
- valid_count: int32 [1], replicated, may hold values from 5120 to 10240
Outputs:
- update: bfloat16 [10240, 5120], P('seq', ('head', 'enc'))
Inputs may be any that keep to these rules, and one draw needn't show every extreme that they name: Key positions from valid_count[0] on are padding and take no weight.
All inputs are finite; a program needn't handle non-finite values.
Results may differ from a plain program's by a relative error of at most 0.015.
The roundings to bfloat16 on the way count: a program that leaves them out, or rounds other values in their place, can miss the bound.
Values may be sent and summed in bfloat16 or wider, within the bound.
No kernel may reach another device: no remote copies, remote signals or barrier semaphores. Data moves between devices by JAX's collectives and lax.ppermute only.
A program may use at most 64 MiB of HBM per device.

v0:
```python
import jax
import jax.numpy as jnp
from jax import lax
from jax.sharding import PartitionSpec as P

HEAD_DIM = 128
epsilon = 1e-06
lowest_score = -1e30


def normalize(matrix, squares, gain_row, feature_count):
    inverse_rms = lax.rsqrt(squares / feature_count + epsilon)
    return (matrix.astype(jnp.float32) * inverse_rms[:, None] * gain_row[None, :]).astype(
        jnp.bfloat16
    )


def absorb(carried, query_heads, key_block, value_block, offset, key_limit):
    running_sum, running_max, running_mass = carried
    scale_factor = query_heads.shape[2] ** (-0.5)
    scores = (
        jnp.einsum("qhd,khd->hqk", query_heads, key_block, preferred_element_type=jnp.float32)
        * scale_factor
    )
    position = offset + jnp.arange(key_block.shape[0], dtype=jnp.int32)
    usable = (position < key_limit)[None, None, :]
    masked = jnp.where(usable, scores, lowest_score)
    new_max = jnp.maximum(running_max, jnp.max(masked, axis=2))
    weights = jnp.where(usable, jnp.exp(masked - new_max[:, :, None]), 0.0)
    factor = jnp.exp(running_max - new_max)
    running_mass = running_mass * factor + jnp.sum(weights, axis=2)
    running_sum = running_sum * factor[:, :, None] + jnp.einsum(
        "hqk,khd->hqd",
        weights.astype(jnp.bfloat16),
        value_block,
        preferred_element_type=jnp.float32,
    )
    return (running_sum, new_max, running_mass)


def absorb_blocks(carried, query_heads, key_rows, value_rows, key_limit):
    row_total = key_rows.shape[0]
    block_size = 512
    block_count = row_total // block_size
    key_blocks = key_rows.reshape((block_count, block_size) + key_rows.shape[1:])
    value_blocks = value_rows.reshape((block_count, block_size) + value_rows.shape[1:])

    def absorb_block(running, triple):
        block_number, key_block, value_block = triple
        return (
            absorb(
                running, query_heads, key_block, value_block, block_number * block_size, key_limit
            ),
            None,
        )

    numbers = jnp.arange(block_count, dtype=jnp.int32)
    carried, _ = lax.scan(absorb_block, carried, (numbers, key_blocks, value_blocks))
    return carried


def visit(carried, query_heads, key_rows, value_rows, key_limit):
    return absorb_blocks(carried, query_heads, key_rows, value_rows, key_limit)


def local(queries, keys, values, out_weight, q_gain, k_gain, gate, valid_count):
    row_count = queries.shape[0]
    local_heads = queries.shape[1] // HEAD_DIM
    feature_count = queries.shape[1] * lax.axis_size(("head", "enc"))
    key_limit = valid_count[0]
    query_squares = jnp.sum(jnp.square(queries.astype(jnp.float32)), axis=1)
    key_squares = jnp.sum(jnp.square(keys.astype(jnp.float32)), axis=1)
    query_totals, key_totals = lax.psum((query_squares, key_squares), ("head", "enc"))
    query_heads = normalize(queries, query_totals, q_gain, feature_count).reshape(
        row_count, local_heads, HEAD_DIM
    )
    key_heads = normalize(keys, key_totals, k_gain, feature_count).reshape(
        row_count, local_heads, HEAD_DIM
    )
    value_heads = values.reshape(row_count, local_heads, HEAD_DIM)
    initial = (
        jnp.zeros((local_heads, row_count, HEAD_DIM), jnp.float32),
        jnp.full((local_heads, row_count), lowest_score, jnp.float32),
        jnp.zeros((local_heads, row_count), jnp.float32),
    )
    running_sum, running_max, running_mass = visit(
        initial,
        query_heads,
        lax.all_gather(key_heads, "seq", axis=0, tiled=True),
        lax.all_gather(value_heads, "seq", axis=0, tiled=True),
        key_limit,
    )
    attended = (running_sum / running_mass[:, :, None]).transpose(1, 0, 2)
    attended = attended.reshape(row_count, local_heads * HEAD_DIM).astype(jnp.bfloat16)
    terms = jnp.dot(
        attended,
        lax.all_gather(out_weight, "seq", axis=1, tiled=True),
        preferred_element_type=jnp.float32,
    )
    summed = lax.psum_scatter(
        terms.astype(jnp.bfloat16), ("head", "enc"), scatter_dimension=1, tiled=True
    ).astype(jnp.float32)
    return (gate[None, :] * summed).astype(jnp.bfloat16)


def solution(mesh):
    placed = (
        P("seq", ("head", "enc")),
        P("seq", ("head", "enc")),
        P("seq", ("head", "enc")),
        P(("head", "enc"), "seq"),
        P(("head", "enc")),
        P(("head", "enc")),
        P(("head", "enc")),
        P(),
    )
    return jax.shard_map(
        local, mesh=mesh, in_specs=placed, out_specs=P("seq", ("head", "enc")), check_vma=False
    )
```

profile of v0, /device:TPU:2, one launch (start us, length us, event | category | flops | bytes accessed | tf_op | source)
XLA Modules:
  0.0 957.6 jit_solution(13073559487828346287)
XLA Ops:
  6.5 1.1 fusion.11
  7.6 1.1 fusion.14
  8.7 78.0 %all-reduce = (f32[320]{0:T(512)S(1)}, f32[320]{0:T(512)S(1)}) all-reduce(f32[320]{0:T(512)S(1)} %fusion.11, f32[320]{0:T(512)S(1)} %fusion.14), channel_id=1, replica_groups=mesh['seq'=32,'head'=8,'enc'=2] {'head','enc'}, use_global_device_ids=true, to_apply=%region_1.0 | all-reduce | flops 640 | bytes 5120 | tf_op jit(solution)/shard_map/psum | solution.py:73
  86.7 1.0 fusion.13
  87.7 0.7 reshape.32
  88.5 1.6 reshape.35
  90.2 0.7 all-gather.8.cloned.1.call-update
  91.1 214.0 %all-gather.4.cloned.1.call-done = bf16[10240,2,128]{2,1,0:T(2,128)(2,1)} async-done(((bf16[320,2,128]{2,1,0:T(2,128)(2,1)}), bf16[10240,2,128]{2,1,0:T(2,128)(2,1)}) %all-gather.4.cloned.1.call-update) | async-done | bytes 5242896 | tf_op jit(solution)/shard_map/all_gather | solution.py:89
  305.2 242.4 %all-gather.6.cloned.1.call-done = bf16[10240,2,128]{2,1,0:T(2,128)(2,1)} async-done(((bf16[320,2,128]{2,1,0:T(2,128)(2,1)}), bf16[10240,2,128]{2,1,0:T(2,128)(2,1)}) %all-gather.6.cloned.1.call-update) | async-done | bytes 5242896 | tf_op jit(solution)/shard_map/all_gather | solution.py:90
  547.6 92.4 %while.15 = (s32[]{:T(128)}, f32[2,320,128]{2,1,0:T(8,128)S(1)}, f32[2,320]{1,0:T(2,128)S(1)}, f32[2,320]{1,0:T(2,128)S(1)}, s32[20]{0:T(128)S(1)}, /*index=5*/s...) while((s32[]{:T(128)}, f32[2,320,128]{2,1,0:T(8,128)S(1)}, ...), condition=%wide.region_7.8_spmd.clone, body=%wide.region_4.7_spmd.clone.sunk | while | flops 170971264 | bytes 6367397 | solution.py:58
  548.8 0.7 add_compare_fusion.2
  549.4 1.4 constant_dynamic-slice_fusion.3
  552.2 0.6 dynamic_slice.19
  553.4 0.7 add_compare_fusion.2
  554.1 1.4 constant_dynamic-slice_fusion.3
  556.8 0.6 dynamic_slice.19
  558.0 0.7 add_compare_fusion.2
  558.7 1.4 constant_dynamic-slice_fusion.3
  561.4 0.6 dynamic_slice.19
  562.7 0.7 add_compare_fusion.2
  563.3 1.4 constant_dynamic-slice_fusion.3
  566.0 0.6 dynamic_slice.19
  567.3 0.7 add_compare_fusion.2
  567.9 1.4 constant_dynamic-slice_fusion.3
  570.7 0.6 dynamic_slice.19
  571.9 0.7 add_compare_fusion.2
  572.6 1.4 constant_dynamic-slice_fusion.3
  575.3 0.6 dynamic_slice.19
  576.5 0.7 add_compare_fusion.2
  577.2 1.4 constant_dynamic-slice_fusion.3
  581.2 0.7 add_compare_fusion.2
  581.8 1.4 constant_dynamic-slice_fusion.3
  585.8 0.7 add_compare_fusion.2
  586.4 1.4 constant_dynamic-slice_fusion.3
  589.2 0.6 dynamic_slice.19
  590.4 0.7 add_compare_fusion.2
  591.1 1.4 constant_dynamic-slice_fusion.3
  593.8 0.6 dynamic_slice.19
  595.0 0.7 add_compare_fusion.2
  595.7 1.4 constant_dynamic-slice_fusion.3
  599.6 0.7 add_compare_fusion.2
  600.3 1.4 constant_dynamic-slice_fusion.3
  604.3 0.7 add_compare_fusion.2
  604.9 1.4 constant_dynamic-slice_fusion.3
  608.9 0.7 add_compare_fusion.2
  609.5 1.4 constant_dynamic-slice_fusion.3
  613.5 0.7 add_compare_fusion.2
  614.2 1.4 constant_dynamic-slice_fusion.3
  618.1 0.7 add_compare_fusion.2
  618.8 1.4 constant_dynamic-slice_fusion.3
  622.8 0.7 add_compare_fusion.2
  623.4 1.4 constant_dynamic-slice_fusion.3
  627.4 0.7 add_compare_fusion.2
  628.0 1.4 constant_dynamic-slice_fusion.3
  632.0 0.7 add_compare_fusion.2
  632.7 1.4 constant_dynamic-slice_fusion.3
  636.6 0.7 add_compare_fusion.2
  637.3 1.4 constant_dynamic-slice_fusion.3
  640.0 136.6 %all-gather.8.cloned.1.call-done = bf16[256,5120]{0,1:T(8,128)(2,1)} async-done(((bf16[256,160]{0,1:T(8,128)(2,1)}), bf16[256,5120]{0,1:T(8,128)(2,1)}) %all-gather.8.cloned.1.call-update) | async-done | bytes 2621456 | tf_op jit(solution)/shard_map/all_gather | solution.py:97
  776.6 2.9 convolution_convert_fusion
  779.6 3.6 copy.29
  783.2 166.0 %reduce-scatter.4.cloned.1.call-done = bf16[320,320]{1,0:T(8,128)(2,1)} async-done(((bf16[5120,320]{1,0:T(8,128)(2,1)}), bf16[320,320]{1,0:T(8,128)(2,1)}) %reduce-scatter.4.cloned.1.call-update) | async-done | bytes 204816
  949.2 1.1 copy.30
  950.4 0.7 multiply_convert_fusion
  (153 shorter events, 33.0 us)
Async XLA Ops:
  6.5 84.5 %copy-start.1 = (bf16[320,256]{1,0:T(8,128)(2,1)S(1)}, bf16[320,256]{1,0:T(8,128)(2,1)}, u32[]{:S(2)}) copy-start(bf16[320,256]{1,0:T(8,128)(2,1)} %param.10) | copy-start | bytes 491524
  6.5 84.5 %copy-start.3 = (f32[256]{0:T(256)S(1)}, f32[256]{0:T(256)}, u32[]{:S(2)}) copy-start(f32[256]{0:T(256)} %param.14) | copy-start | bytes 3076
  6.5 298.6 %all-gather.4.cloned.1.call-start = ((), (), s32[]{:S(2)}) async-start(), calls=%async_computation.1 | async-start | bytes 5406720 | tf_op jit(solution)/shard_map/all_gather | solution.py:89
  88.5 459.1 %all-gather.6.cloned.1.call-start = ((), (), s32[]{:S(2)}) async-start(), calls=%async_computation.2 | async-start | bytes 5406720 | tf_op jit(solution)/shard_map/all_gather | solution.py:90
  90.2 686.4 %all-gather.8.cloned.1.call-start = ((), (), s32[]{:S(2)}) async-start(), calls=%async_computation.3 | async-start | bytes 2703360 | tf_op jit(solution)/shard_map/all_gather | solution.py:97
  90.9 858.3 %reduce-scatter.4.cloned.1.call-start = ((), (), s32[]{:S(2)}) async-start(), calls=%async_computation.4 | async-start | bytes 4177920
  640.0 136.6 %copy-start = (f32[2,320,128]{2,1,0:T(8,128)}, f32[2,320,128]{2,1,0:T(8,128)S(1)}, u32[]{:S(2)}) copy-start(f32[2,320,128]{2,1,0:T(8,128)S(1)} %get-tuple-element.53) | copy-start | bytes 983044
  783.2 167.2 %copy-start.2 = (f32[320]{0:T(512)S(1)}, f32[320]{0:T(512)}, u32[]{:S(2)}) copy-start(f32[320]{0:T(512)} %param.16) | copy-start | bytes 3844
Sparse Core Ops, SparseCore 0:
  88.6 216.5 all-gather.3
  307.2 240.2 all-gather.5
  549.6 226.9 all-gather.7
  783.4 165.8 reduce-scatter.3
where the time goes:
time: 959 us; the launch traced here: 958 us
  waiting for transfers between devices  760 us (79%)
  blocking collectives  78 us (8%)
  local copies, waits for them, and re-layouts  46.8 us (5%)
  other arithmetic  25.5 us (3%)
  matrix products  20.2 us (2%)
  loops' own time  14.1 us (1%)
  between operations  13.2 us (1%)
    all_gather x1, waiting for transfers between devices, local(): lax.all_gather(value_heads, 'seq', axis=0, tiled=True)  242 us
    all_gather x1, waiting for transfers between devices, local(): lax.all_gather(key_heads, 'seq', axis=0, tiled=True)  214 us
    unnamed x5, waiting for transfers between devices  167 us
    all_gather x1, waiting for transfers between devices, local(): lax.all_gather(out_weight, 'seq', axis=1, tiled=True)  137 us
    psum x1, blocking collectives, local(): lax.psum((query_squares, key_squares), ('head', 'enc'))  78 us
    dynamic_slice x40, local copies, waits for them, and re-layouts, absorb_blocks(): lax.scan(absorb_block, carried, (numbers, key_blocks, value_blocks))  39.7 us
  transfers between devices with their start and end apart: 4, of which 4 were waited for; matrix products, arithmetic and copies ran while one was open for 8% of the time, Pallas kernels for 0%

commit v1 on v0

--- a/solution.py
+++ b/solution.py
@@ -70,7 +70,7 @@
     key_limit = valid_count[0]
     query_squares = jnp.sum(jnp.square(queries.astype(jnp.float32)), axis=1)
     key_squares = jnp.sum(jnp.square(keys.astype(jnp.float32)), axis=1)
-    query_totals, key_totals = lax.psum((query_squares, key_squares), ("head", "enc"))
+    query_totals, key_totals = lax.psum(lax.psum((query_squares, key_squares), "head"), "enc")
     query_heads = normalize(queries, query_totals, q_gain, feature_count).reshape(
         row_count, local_heads, HEAD_DIM
     )

time: 959 us -> 918 us (0.957)
  blocking collectives: 78 us -> 31.6 us
    psum x1 -> x2, blocking collectives: 78 us -> 31.6 us  [the longest x1 16.7 us: local(): lax.psum(lax.psum((query_squares, key_squares), 'head'), 'enc')]
  transfers between devices with their start and end apart: 4 -> 4, of which waited for: 4 -> 4; matrix products, arithmetic and copies ran while one was open for 8% -> 9% of each run, Pallas kernels for 0% -> 0%
where the time goes in v1:
time: 918 us; the launch traced here: 917 us
  waiting for transfers between devices  766 us (83%)
  local copies, waits for them, and re-layouts  46.8 us (5%)
  blocking collectives  31.6 us (3%)
  other arithmetic  24.5 us (3%)
  matrix products  20.2 us (2%)
  loops' own time  14.1 us (2%)
  between operations  13.2 us (1%)
    all_gather x1, waiting for transfers between devices, local(): lax.all_gather(value_heads, 'seq', axis=0, tiled=True)  242 us
    all_gather x1, waiting for transfers between devices, local(): lax.all_gather(key_heads, 'seq', axis=0, tiled=True)  221 us
    unnamed x5, waiting for transfers between devices  166 us
    all_gather x1, waiting for transfers between devices, local(): lax.all_gather(out_weight, 'seq', axis=1, tiled=True)  137 us
    dynamic_slice x40, local copies, waits for them, and re-layouts, absorb_blocks(): lax.scan(absorb_block, carried, (numbers, key_blocks, value_blocks))  39.7 us
  transfers between devices with their start and end apart: 4, of which 4 were waited for; matrix products, arithmetic and copies ran while one was open for 9% of the time, Pallas kernels for 0%

profile of v1, /device:TPU:2, one launch (start us, length us, event | category | flops | bytes accessed | tf_op | source)
XLA Modules:
  0.0 916.9 jit_solution(6728783029805374470)
XLA Ops:
  6.5 1.2 fusion.11
  7.8 14.9 %all-reduce = (f32[320]{0:T(512)S(1)}, f32[320]{0:T(512)S(1)}) all-reduce(f32[320]{0:T(512)S(1)} %get-tuple-element.140, f32[320]{0:T(512)S(1)} %get-tuple-element.141), channel_id=1, replica_groups=mesh['seq'=32,'head'=8,'enc'=2] {'head'}, use_global_device_ids=true, to_apply=%region_1.0 | all-reduce | flops 640 | bytes 5120 | tf_op jit(solution)/shard_map/psum | solution.py:73
  22.6 16.7 %all-reduce.1 = (f32[320]{0:T(512)S(1)}, f32[320]{0:T(512)S(1)}) all-reduce(f32[320]{0:T(512)S(1)} %get-tuple-element.130, f32[320]{0:T(512)S(1)} %get-tuple-element.131), channel_id=1, replica_groups=mesh['seq'=32,'head'=8,'enc'=2] {'enc'}, use_global_device_ids=true, to_apply=%region_2.0 | all-reduce | flops 640 | bytes 5120 | tf_op jit(solution)/shard_map/psum | solution.py:73
  39.3 1.0 fusion.13
  40.4 0.7 reshape.32
  41.2 1.6 reshape.35
  42.8 0.7 all-gather.8.cloned.1.call-update
  43.8 221.2 %all-gather.4.cloned.1.call-done = bf16[10240,2,128]{2,1,0:T(2,128)(2,1)} async-done(((bf16[320,2,128]{2,1,0:T(2,128)(2,1)}), bf16[10240,2,128]{2,1,0:T(2,128)(2,1)}) %all-gather.4.cloned.1.call-update) | async-done | bytes 5242896 | tf_op jit(solution)/shard_map/all_gather | solution.py:89
  264.9 242.4 %all-gather.6.cloned.1.call-done = bf16[10240,2,128]{2,1,0:T(2,128)(2,1)} async-done(((bf16[320,2,128]{2,1,0:T(2,128)(2,1)}), bf16[10240,2,128]{2,1,0:T(2,128)(2,1)}) %all-gather.6.cloned.1.call-update) | async-done | bytes 5242896 | tf_op jit(solution)/shard_map/all_gather | solution.py:90
  507.3 92.4 %while.15 = (s32[]{:T(128)}, f32[2,320,128]{2,1,0:T(8,128)S(1)}, f32[2,320]{1,0:T(2,128)S(1)}, f32[2,320]{1,0:T(2,128)S(1)}, s32[20]{0:T(128)S(1)}, /*index=5*/s...) while((s32[]{:T(128)}, f32[2,320,128]{2,1,0:T(8,128)S(1)}, ...), condition=%wide.region_9.10_spmd.clone, body=%wide.region_6.9_spmd.clone.sunk | while | flops 170971264 | bytes 6367397 | solution.py:58
  508.6 0.7 add_compare_fusion.2
  509.2 1.4 constant_dynamic-slice_fusion.3
  511.9 0.6 dynamic_slice.19
  513.2 0.7 add_compare_fusion.2
  513.8 1.4 constant_dynamic-slice_fusion.3
  516.6 0.6 dynamic_slice.19
  517.8 0.7 add_compare_fusion.2
  518.4 1.4 constant_dynamic-slice_fusion.3
  522.4 0.7 add_compare_fusion.2
  523.1 1.4 constant_dynamic-slice_fusion.3
  525.8 0.6 dynamic_slice.19
  527.0 0.7 add_compare_fusion.2
  527.7 1.4 constant_dynamic-slice_fusion.3
  530.4 0.6 dynamic_slice.19
  531.7 0.7 add_compare_fusion.2
  532.3 1.4 constant_dynamic-slice_fusion.3
  535.0 0.6 dynamic_slice.19
  536.3 0.7 add_compare_fusion.2
  536.9 1.4 constant_dynamic-slice_fusion.3
  539.7 0.6 dynamic_slice.19
  540.9 0.7 add_compare_fusion.2
  541.6 1.4 constant_dynamic-slice_fusion.3
  544.3 0.6 dynamic_slice.19
  545.5 0.7 add_compare_fusion.2
  546.2 1.4 constant_dynamic-slice_fusion.3
  548.9 0.6 dynamic_slice.19
  550.2 0.7 add_compare_fusion.2
  550.8 1.4 constant_dynamic-slice_fusion.3
  554.8 0.7 add_compare_fusion.2
  555.4 1.4 constant_dynamic-slice_fusion.3
  559.4 0.7 add_compare_fusion.2
  560.1 1.4 constant_dynamic-slice_fusion.3
  564.0 0.7 add_compare_fusion.2
  564.7 1.4 constant_dynamic-slice_fusion.3
  568.6 0.7 add_compare_fusion.2
  569.3 1.4 constant_dynamic-slice_fusion.3
  573.3 0.7 add_compare_fusion.2
  573.9 1.4 constant_dynamic-slice_fusion.3
  577.9 0.7 add_compare_fusion.2
  578.6 1.4 constant_dynamic-slice_fusion.3
  582.5 0.7 add_compare_fusion.2
  583.2 1.4 constant_dynamic-slice_fusion.3
  587.1 0.7 add_compare_fusion.2
  587.8 1.4 constant_dynamic-slice_fusion.3
  591.8 0.7 add_compare_fusion.2
  592.4 1.4 constant_dynamic-slice_fusion.3
  596.4 0.7 add_compare_fusion.2
  597.0 1.4 constant_dynamic-slice_fusion.3
  599.8 137.2 %all-gather.8.cloned.1.call-done = bf16[256,5120]{0,1:T(8,128)(2,1)} async-done(((bf16[256,160]{0,1:T(8,128)(2,1)}), bf16[256,5120]{0,1:T(8,128)(2,1)}) %all-gather.8.cloned.1.call-update) | async-done | bytes 2621456 | tf_op jit(solution)/shard_map/all_gather | solution.py:97
  737.0 2.9 convolution_convert_fusion
  739.9 3.6 copy.29
  743.6 165.0 %reduce-scatter.4.cloned.1.call-done = bf16[320,320]{1,0:T(8,128)(2,1)} async-done(((bf16[5120,320]{1,0:T(8,128)(2,1)}), bf16[320,320]{1,0:T(8,128)(2,1)}) %reduce-scatter.4.cloned.1.call-update) | async-done | bytes 204816
  908.5 1.1 copy.30
  909.7 0.7 multiply_convert_fusion
  (154 shorter events, 33.0 us)
Async XLA Ops:
  6.5 37.1 %copy-start.1 = (bf16[320,256]{1,0:T(8,128)(2,1)S(1)}, bf16[320,256]{1,0:T(8,128)(2,1)}, u32[]{:S(2)}) copy-start(bf16[320,256]{1,0:T(8,128)(2,1)} %param.10) | copy-start | bytes 491524
  6.5 37.1 %copy-start.3 = (f32[256]{0:T(256)S(1)}, f32[256]{0:T(256)}, u32[]{:S(2)}) copy-start(f32[256]{0:T(256)} %param.14) | copy-start | bytes 3076
  6.5 258.4 %all-gather.4.cloned.1.call-start = ((), (), s32[]{:S(2)}) async-start(), calls=%async_computation.1 | async-start | bytes 5406720 | tf_op jit(solution)/shard_map/all_gather | solution.py:89
  41.1 466.2 %all-gather.6.cloned.1.call-start = ((), (), s32[]{:S(2)}) async-start(), calls=%async_computation.2 | async-start | bytes 5406720 | tf_op jit(solution)/shard_map/all_gather | solution.py:90
  42.8 694.2 %all-gather.8.cloned.1.call-start = ((), (), s32[]{:S(2)}) async-start(), calls=%async_computation.3 | async-start | bytes 2703360 | tf_op jit(solution)/shard_map/all_gather | solution.py:97
  43.5 865.0 %reduce-scatter.4.cloned.1.call-start = ((), (), s32[]{:S(2)}) async-start(), calls=%async_computation.4 | async-start | bytes 4177920
  599.8 137.2 %copy-start = (f32[2,320,128]{2,1,0:T(8,128)}, f32[2,320,128]{2,1,0:T(8,128)S(1)}, u32[]{:S(2)}) copy-start(f32[2,320,128]{2,1,0:T(8,128)S(1)} %get-tuple-element.53) | copy-start | bytes 983044
  743.5 166.1 %copy-start.2 = (f32[320]{0:T(512)S(1)}, f32[320]{0:T(512)}, u32[]{:S(2)}) copy-start(f32[320]{0:T(512)} %param.16) | copy-start | bytes 3844
Sparse Core Ops, SparseCore 0:
  41.2 223.6 all-gather.3
  267.0 240.2 all-gather.5
  509.4 227.5 all-gather.7
  743.7 164.7 reduce-scatter.3
